TPU v7x, 256 devices: a whole 4x4x8 slice. The times are simulated.
256 devices in a mesh: pipe: 4 (over x), seq: 64 (over z, y, core).
Axes of the slice: x: 4, y: 4, z: 8, core: 2. Of those that a mesh axis runs over, the one named last changes fastest.
Arguments:
- query_latent: bfloat16 [4, 1024, 64, 512], P('pipe', 'seq'), may hold values from -32 to 32
- query_rope: bfloat16 [4, 1024, 4096], P('pipe', 'seq'), may hold values from -4 to 4
- key_latent: bfloat16 [4, 1024, 512], P('pipe', 'seq'), may hold values from -8 to 8
- key_rope: bfloat16 [4, 1024, 64], P('pipe', 'seq'), may hold values from -4 to 4
- positions: int32 [4, 1024], P('pipe', 'seq'), may hold values from -1 to 8191, as said below
- router_weight: float32 [4, 1024], P('pipe', 'seq'), may hold values from 0.2 to 1
- value_up: bfloat16 [4, 64, 512, 128], P('pipe'), may hold values from -1.5 to 1.5
Outputs:
- handed: bfloat16 [4, 1024, 8192], P('pipe', 'seq')
Inputs may be any that keep to these rules, and one draw needn't show every extreme that they name: Within a section, each device's block of 16 slots (the device with seq index i holds positions in [i * 128, (i + 1) * 128)) has its live rows first, positions strictly rising, then empty slots holding -1. At least 8 slots of every block are live, and in every section some block has all 16 slots live.
All inputs are finite; a program needn't handle non-finite values.
Results may differ from a plain program's by a relative error of at most 0.007.
Values may be sent and summed in bfloat16 or wider, within the bound.
A program may use at most 64 MiB of HBM per device.

v0:
```python
import jax
import jax.numpy as jnp
from jax import lax
from jax.sharding import PartitionSpec as P

SOFTMAX_SCALE = 0.07216878364870322
MASKED = -1e30


def passed_along(block, axis, distance):
    devices = range(lax.axis_size(axis))
    route = [((i - distance) % len(devices), i) for i in devices]
    return lax.ppermute(block, axis, route)


def block_scores(query_block, rope_block, key_block, key_rope_block, query_pos, key_pos):
    scores = jnp.einsum("qhl,kl->qhk", query_block, key_block, preferred_element_type=jnp.float32)
    scores = scores + jnp.einsum(
        "qhr,kr->qhk", rope_block, key_rope_block, preferred_element_type=jnp.float32
    )
    scores = scores * SOFTMAX_SCALE
    visible = (key_pos[None, :] >= 0) & (key_pos[None, :] <= query_pos[:, None])
    return (jnp.where(visible[:, None, :], scores, MASKED), visible)


def on_device(query_latent, query_rope, key_latent, key_rope, positions, router_weight, value_up):
    row_count = query_latent.shape[1]
    head_count = query_latent.shape[2]
    lat_width = query_latent.shape[3]
    query_local = query_latent[0]
    rope_local = query_rope[0].reshape(row_count, head_count, -1)
    own_pos = positions[0]
    start_state = (
        jnp.full((row_count, head_count), MASKED, jnp.float32),
        jnp.zeros((row_count, head_count), jnp.float32),
        jnp.zeros((row_count, head_count, lat_width), jnp.float32),
    )
    piece_latent = lax.all_gather(key_latent, "seq", axis=1, tiled=True)
    piece_rope = lax.all_gather(key_rope, "seq", axis=1, tiled=True)
    piece_pos = lax.all_gather(positions, "seq", axis=1, tiled=True)
    scores, visible = block_scores(
        query_local, rope_local, piece_latent[0], piece_rope[0], own_pos, piece_pos[0]
    )

    def update_state(state):
        run_max, run_sum, accumulated = state
        new_max = jnp.maximum(run_max, jnp.max(scores, axis=2))
        weights = jnp.where(visible[:, None, :], jnp.exp(scores - new_max[:, :, None]), 0.0)
        new_sum = jnp.sum(weights, axis=2)
        update = jnp.einsum(
            "qhk,kl->qhl",
            weights.astype(jnp.bfloat16),
            piece_latent[0],
            preferred_element_type=jnp.float32,
        )
        return (new_max, new_sum, update)

    def keep_state(state):
        return state

    run_max, run_sum, accumulated = lax.cond(
        jnp.any(visible), update_state, keep_state, start_state
    )
    latent = (accumulated / jnp.maximum(run_sum, 1.0)[:, :, None]).astype(jnp.bfloat16)
    projected = jnp.einsum("qhl,hlv->qhv", latent, value_up[0], preferred_element_type=jnp.float32)
    result = (projected.reshape(row_count, -1) * router_weight[0][:, None]).astype(jnp.bfloat16)
    handed = passed_along(result, "pipe", 1)
    return handed[None]


def solution(mesh):
    placed = (
        P("pipe", "seq", None, None),
        P("pipe", "seq", None),
        P("pipe", "seq", None),
        P("pipe", "seq", None),
        P("pipe", "seq"),
        P("pipe", "seq"),
        P("pipe", None, None, None),
    )
    return jax.shard_map(
        on_device, mesh=mesh, in_specs=placed, out_specs=P("pipe", "seq", None), check_vma=False
    )
```

profile of v0, /device:TPU:1, one launch (start us, length us, event | category | flops | bytes accessed | tf_op | source)
XLA Modules:
  0.0 118.8 jit_solution(2066651595685825759)
XLA Ops:
  6.5 0.0 copy-start
  6.5 0.0 all-gather.2.cloned.1.call-start
  6.5 0.7 all-gather.2.cloned.1.call-update
  7.3 1.3 %dynamic-slice = u32[1]{0:T(128)} dynamic-slice(u32[256]{0:T(256)} %constant.34, u32[]{:T(128)S(6)} %add.5), dynamic_slice_sizes={1} | dynamic-slice | bytes 12
  9.2 0.8 bitcast_dynamic-update-slice_fusion
  10.0 20.7 %all-reduce = s32[1024]{0:T(1024)S(1)} all-reduce(s32[1024]{0:T(1024)S(1)} %bitcast_dynamic-update-slice_fusion), channel_id=1, replica_groups=mesh['pipe'=4,'seq'=64] {'seq'}, use_global_device_ids=true, to_apply=%add | all-reduce | flops 1024 | bytes 8192 | tf_op jit(solution)/shard_map/le | solution.py:22
  30.7 1.4 %fusion.22 = (pred[]{:T(512)}, pred[16,1024]{1,0:T(8,128)(4,1)S(1)}) fusion(s32[16]{0:T(128)} %bitcast.35, s32[1024]{0:T(1024)S(1)} %all-reduce, pred[1024]{0:T(1024)(128)(4,1)S(1)} %broadcast_compare_fusion), kind=kLoop, calls=%fused_computation.29 | loop fusion | flops 49151 | bytes 21569 | tf_op jit(solution)/shard_map/reduce_or | solution.py:62
  32.7 1.2 reshape_squeeze.3
  33.9 46.5 %all_gather.11 = bf16[1,1024,64]{2,1,0:T(8,128)(2,1)S(1)} all-gather(bf16[1,16,64]{2,1,0:T(8,128)(2,1)} %param.12), channel_id=1, replica_groups=mesh['pipe'=4,'seq'=64] {'seq'}, dimensions={1}, use_global_device_ids=true | all-gather | bytes 133120 | tf_op jit(solution)/shard_map/all_gather | solution.py:39
  80.4 2.6 %fusion.19 = f32[16,64,1024]{2,1,0:T(8,128)} fusion(bf16[16,64,64]{2,1,0:T(8,128)(2,1)S(1)} %reshape_squeeze.3, bf16[1,1024,64]{2,1,0:T(8,128)(2,1)S(1)} %all_gather.11), kind=kOutput, calls=%fused_computation.22 | convolution fusion | flops 134217728 | bytes 4456448 | tf_op jit(solution)/shard_map/qhr,kr->qhk/dot_general | solution.py:18
  83.1 0.0 copy-start.3
  83.1 7.7 %all-gather.2.cloned.1.call-done = bf16[1,1024,512]{2,1,0:T(8,128)(2,1)} async-done(((bf16[1,16,512]{2,1,0:T(8,128)(2,1)}), bf16[1,1024,512]{2,1,0:T(8,128)(2,1)}) %all-gather.2.cloned.1.call-update) | async-done | bytes 1048592 | tf_op jit(solution)/shard_map/all_gather | solution.py:38
  90.7 0.0 copy-done
  90.7 0.0 copy-start.1
  90.7 0.0 copy-start.2
  90.7 2.7 %fusion.14 = f32[16,64,1024]{2,1,0:T(8,128)S(1)} fusion(bf16[1,1024,512]{2,1,0:T(8,128)(2,1)} %all-gather.2.cloned.1.call-done, bf16[1,16,64,512]{3,2,1,0:T(8,128)(2,1)S(1)} %copy-done), kind=kOutput, calls=%fused_computation.16 | convolution fusion | flops 1073741824 | bytes 6291456 | tf_op jit(solution)/shard_map/qhl,kl->qhk/dot_general | solution.py:17
  93.4 0.0 copy-done.3
  93.4 0.0 copy-done.1
  93.4 0.1 copy-done.2
  93.5 3.3 %conditional.1 = (f32[16,64]{1,0:T(8,128)S(1)}, f32[16,64,512]{2,1,0:T(8,128)S(1)}) conditional(s32[]{:T(128)} %convert_element_type.13, () %tuple.27, (pred[16,1024]{1,0:T(8,128)(4,1)S(1)}, pred[1024]{0:T(1024)(128)(4,1)S(1)}, s32[1024]{0:T(1024)S(1)}, s32[16]{0:T(128)S(1)}, f32[16,64,1024]{2,1,0:T(8,128)S(1)}, ...), branch_computations={%region_1.2_spmd, %region_2.5_spmd} | conditional | flops 1084259328 | bytes 24212560 | solution.py:61
  93.5 0.1 compare_and_fusion
  93.6 0.8 fusion.21
  94.4 1.1 fusion.1
  95.5 1.3 %fusion.2 = f32[16,64,512]{2,1,0:T(8,128)S(1)} fusion(f32[16,64,1024]{2,1,0:T(8,128)S(1)} %get-tuple-element.59, f32[16,64]{1,0:T(8,128)S(1)} %broadcast_maximum_fusion, pred[16,1024]{1,0:T(8,128)(4,1)S(1)} %get-tuple-element.47, bf16[1,1024,512]{2,1,0:T(8,128)(2,1)S(1)} %get-tuple-element.53), kind=kOutput, calls=%fused_computation.4 | convolution fusion | flops 1076887552 | bytes 7360512 | tf_op jit(solution)/shard_map/cond/branch_1_fun/qhk,kl->qhl/dot_general | solution.py:50
  96.9 0.2 divide_convert_fusion
  97.1 0.0 copy-start.4
  97.1 5.1 %fusion.11 = f32[64,2,8,128]{3,2,1,0:T(8,128)S(1)} fusion(bf16[1,64,512,128]{3,2,1,0:T(8,128)(2,1)} %param.15, bf16[16,64,512]{2,1,0:T(8,128)(2,1)S(1)} %divide_convert_fusion), kind=kOutput, calls=%fused_computation.15 | convolution fusion | flops 134217728 | bytes 9961472 | tf_op jit(solution)/shard_map/qhl,hlv->qhv/dot_general | solution.py:65
  102.2 0.0 copy-done.4
  102.2 0.1 fusion.18
  102.3 1.3 %collective-permute-start = (bf16[16,8192]{1,0:T(8,128)(2,1)S(1)}, bf16[16,8192]{1,0:T(8,128)(2,1)S(1)}, u32[]{:S(2)}, u32[]{:S(2)}) collective-permute-start(bf16[16,8192]{1,0:T(8,128)(2,1)S(1)} %fusion.18), channel_id=1, source_target_pairs={{192,0},{0,64},{64,128},{128,192},{193,1},{1,65},{65,129},{129,193... | collective-permute-start | bytes 786440 | tf_op jit(solution)/shard_map/ppermute | solution.py:13
  103.6 7.7 %collective-permute-done = bf16[16,8192]{1,0:T(8,128)(2,1)S(1)} collective-permute-done((bf16[16,8192]{1,0:T(8,128)(2,1)S(1)}, bf16[16,8192]{1,0:T(8,128)(2,1)S(1)}, u32[]{:S(2)}, u32[]{:S(2)}) %collective-permute-start) | collective-permute-done | bytes 262176 | tf_op jit(solution)/shard_map/ppermute | solution.py:13
  111.3 0.7 copy.26
  (4 shorter events, 0.0 us)
Async XLA Ops:
  6.5 84.2 %copy-start = (bf16[1,16,64,512]{3,2,1,0:T(8,128)(2,1)S(1)}, bf16[1,16,64,512]{3,2,1,0:T(8,128)(2,1)}, u32[]{:S(2)}) copy-start(bf16[1,16,64,512]{3,2,1,0:T(8,128)(2,1)} %param.9) | copy-start | bytes 3145732
  6.5 84.2 %all-gather.2.cloned.1.call-start = ((), (), s32[]{:S(2)}) async-start(), calls=%async_computation | async-start | bytes 1064960 | tf_op jit(solution)/shard_map/all_gather | solution.py:38
  83.1 10.3 %copy-start.3 = (s32[1,16]{1,0:T(1,128)S(1)}, s32[1,16]{1,0:T(1,128)}, u32[]{:S(2)}) copy-start(s32[1,16]{1,0:T(1,128)} %param.13) | copy-start | bytes 196
  90.7 2.7 %copy-start.1 = (f32[16,64,1024]{2,1,0:T(8,128)S(1)}, f32[16,64,1024]{2,1,0:T(8,128)}, u32[]{:S(2)}) copy-start(f32[16,64,1024]{2,1,0:T(8,128)} %fusion.19) | copy-start | bytes 12582916
  90.7 2.8 %copy-start.2 = (bf16[1,1024,512]{2,1,0:T(8,128)(2,1)S(1)}, bf16[1,1024,512]{2,1,0:T(8,128)(2,1)}, u32[]{:S(2)}) copy-start(bf16[1,1024,512]{2,1,0:T(8,128)(2,1)} %all-gather.2.cloned.1.call-done) | copy-start | bytes 3145732
  97.1 5.1 %copy-start.4 = (f32[1,16]{1,0:T(1,128)S(1)}, f32[1,16]{1,0:T(1,128)}, u32[]{:S(2)}) copy-start(f32[1,16]{1,0:T(1,128)} %param.14) | copy-start | bytes 196
  102.3 9.0 %collective-permute-start = (bf16[16,8192]{1,0:T(8,128)(2,1)S(1)}, bf16[16,8192]{1,0:T(8,128)(2,1)S(1)}, u32[]{:S(2)}, u32[]{:S(2)}) collective-permute-start(bf16[16,8192]{1,0:T(8,128)(2,1)S(1)} %fusion.18), channel_id=1, source_target_pairs={{192,0},{0,64},{64,128},{128,192},{193,1},{1,65},{65,129},{129,193... | collective-permute-start | bytes 786440 | tf_op jit(solution)/shard_map/ppermute | solution.py:13
Sparse Core Ops, SparseCore 0:
  10.1 80.5 all-gather.1
where the time goes:
time: 119 us
  blocking collectives  67.2 us (56%)
  waiting for transfers between devices  16 us (13%)
  between operations  14.8 us (12%)
  matrix products  11.7 us (10%)
  local copies, waits for them, and re-layouts  4.06 us (3%)
  other arithmetic  3.7 us (3%)
  starting transfers between devices  1.29 us (1%)
    all_gather x1, blocking collectives, on_device(): piece_rope = lax.all_gather(key_rope, 'seq', axis=1, tiled=True)  46.5 us
    le x1, blocking collectives, block_scores(): visible = (key_pos[None, :] >= 0) & (key_pos[None, :] <= query_pos[:, None])  20.7 us
    ppermute x1, waiting for transfers between devices, passed_along(): return lax.ppermute(block, axis, route)  7.67 us
    all_gather x1, waiting for transfers between devices, on_device(): piece_latent = lax.all_gather(key_latent, 'seq', axis=1, tiled=True)  7.66 us
    dot_general x1, matrix products, on_device(): jnp.einsum('qhl,hlv->qhv', latent, value_up[0], preferred_element_type=jn...  5.09 us
    unnamed x14, local copies, waits for them, and re-layouts  2.88 us
    dot_general x1, matrix products, block_scores(): jnp.einsum('qhl,kl->qhk', query_block, key_block, preferred_element_type=...  2.65 us
    dot_general x1, matrix products, block_scores(): jnp.einsum('qhr,kr->qhk', rope_block, key_rope_block, preferred_element_t...  2.64 us
  transfers between devices with their start and end apart: 2, of which 2 were waited for; matrix products, arithmetic and copies ran while one was open for 6% of the time, Pallas kernels for 0%

commit v1 on v0

v1 whole, which is shorter than its diff:
```python
import jax
import jax.numpy as jnp
from jax import lax
from jax.experimental import pallas as pl
from jax.experimental.pallas import tpu as pltpu
from jax.sharding import PartitionSpec as P

SCALE_LOG2E = 0.07216878364870322 * 1.4426950408889634
MASKED = -1.0e30
ROWS = 16
HEADS = 64
LAT = 512
ROPE = 64
VD = 128
NZ = 8
NY = 4
WIDE = LAT + 128
ZROW = NY * 2 * ROWS
KEYS = NZ * ZROW
GROUP = 16
GROUP_ROWS = GROUP * ROWS
N_GROUPS = HEADS // GROUP
PIECE = 4
MESH = pl.DeviceIdType.MESH
PLACE = {0: 0, 7: 1, 1: 2, 6: 3, 2: 4, 5: 5, 3: 6, 4: 7}
NEAR_FIRST = (7, 1, 6, 2, 5, 3, 4)


def body(
    ql_hbm, qr_hbm, kl_hbm, kr_hbm, pos_hbm, rw_hbm, vu_hbm, out_hbm,
    ql, qr, kl, kr, pos, rw, vu, q, kv, res,
    local_sem, vu_sem, a_send, a_recv, y_send, y_recv, c_send, c_recv, x_send, x_recv,
):
    seq = lax.axis_index("seq")
    pipe = lax.axis_index("pipe")
    z = seq // (NY * 2)
    y = (seq // 2) % NY
    c = seq % 2

    def at(zz, yy, cc):
        return {"seq": (zz * NY + yy) * 2 + cc}

    def y_peer(dy):
        return at(z, (y + dy) % NY, c)

    sibling = at(z, y, 1 - c)
    after = {"pipe": (pipe + 1) % 4}
    before = {"pipe": (pipe + 3) % 4}

    barrier = pltpu.get_barrier_semaphore()
    for t in range(1, NZ):

        @pl.when(z - t >= 0)
        def _():
            pl.semaphore_signal(barrier, inc=1, device_id=at(z - t, y, c), device_id_type=MESH)

    for dy in (1, 2, 3):
        pl.semaphore_signal(barrier, inc=1, device_id=y_peer(dy), device_id_type=MESH)
    pl.semaphore_signal(barrier, inc=1, device_id=sibling, device_id_type=MESH)
    pl.semaphore_signal(barrier, inc=1, device_id=before, device_id_type=MESH)

    loads = [
        pltpu.make_async_copy(kl_hbm.at[0], kl, local_sem.at[0]),
        pltpu.make_async_copy(kr_hbm.at[0], kr, local_sem.at[1]),
        pltpu.make_async_copy(pos_hbm, pos, local_sem.at[2]),
        pltpu.make_async_copy(rw_hbm, rw, local_sem.at[3]),
        pltpu.make_async_copy(ql_hbm.at[0], ql, local_sem.at[4]),
        pltpu.make_async_copy(qr_hbm.at[0], qr, local_sem.at[5]),
    ]
    for load in loads:
        load.start()

    def vu_load(g):
        return pltpu.make_async_copy(
            vu_hbm.at[0, pl.ds(g * GROUP, GROUP)], vu.at[pl.ds(g * GROUP, GROUP)], vu_sem.at[g]
        )

    diagonal = lax.broadcasted_iota(jnp.int32, (ROWS, ROWS), 0) == lax.broadcasted_iota(
        jnp.int32, (ROWS, ROWS), 1
    )
    for load in loads[:4]:
        load.wait()
    live_lane = jnp.where(pos[...] >= 0, 1.0, 0.0)
    live = jnp.sum(jnp.where(diagonal, live_lane, 0.0), axis=1, keepdims=True)
    gate = jnp.sum(jnp.where(diagonal, rw[...], 0.0), axis=1, keepdims=True) * live
    lane = lax.broadcasted_iota(jnp.int32, (ROWS, 128), 1)
    bias = jnp.where(live > 0.5, 0.0, MASKED)
    place = c * (NY * ROWS) + y * ROWS
    own_rows = pl.ds(pl.multiple_of(place, ROWS), ROWS)
    kv[own_rows, :LAT] = kl[...]
    kv[own_rows, LAT:] = jnp.where(
        lane < ROPE,
        jnp.concatenate([kr[...].astype(jnp.float32), jnp.zeros((ROWS, 128 - ROPE), jnp.float32)], axis=1),
        jnp.where(lane == ROPE, bias, 0.0),
    ).astype(jnp.bfloat16)

    pl.semaphore_wait(barrier, (NZ - 1 - z) + 5)

    def rows_of(dz):
        return pl.ds(pl.multiple_of(PLACE[dz] * ZROW + place, ROWS), ROWS)

    def half_of(dz, cc):
        return pl.ds(pl.multiple_of(PLACE[dz] * ZROW + cc * (NY * ROWS), ROWS), NY * ROWS)

    def a_copy(t):
        return pltpu.make_async_remote_copy(
            src_ref=kv.at[own_rows],
            dst_ref=kv.at[rows_of(NZ - t)],
            send_sem=a_send.at[t - 1],
            recv_sem=a_recv.at[NZ - t - 1],
            device_id=at(z + t, y, c),
            device_id_type=MESH,
        )

    def a_arrival(dz):
        return pltpu.make_async_remote_copy(
            src_ref=kv.at[own_rows],
            dst_ref=kv.at[rows_of(dz)],
            send_sem=a_send.at[0],
            recv_sem=a_recv.at[dz - 1],
            device_id=sibling,
            device_id_type=MESH,
        )

    def y_copy(dz, dy):
        return pltpu.make_async_remote_copy(
            src_ref=kv.at[rows_of(dz)],
            dst_ref=kv.at[rows_of(dz)],
            send_sem=y_send.at[dz, dy - 1],
            recv_sem=y_recv.at[dz, dy - 1],
            device_id=y_peer(dy),
            device_id_type=MESH,
        )

    def c_copy(dz):
        return pltpu.make_async_remote_copy(
            src_ref=kv.at[half_of(dz, c)],
            dst_ref=kv.at[half_of(dz, c)],
            send_sem=c_send.at[dz],
            recv_sem=c_recv.at[dz],
            device_id=sibling,
            device_id_type=MESH,
        )

    for t in (1, 2, 3, 4, 5, 6, 7):

        @pl.when(z + t < NZ)
        def _():
            a_copy(t).start()

    for dy in (1, 3, 2):
        y_copy(0, dy).start()
    for g in range(N_GROUPS):
        vu_load(g).start()

    tail_tile = jnp.where(lax.broadcasted_iota(jnp.int32, (ZROW, 128), 1) == ROPE, MASKED, 0.0).astype(jnp.bfloat16)
    for dz in NEAR_FIRST:

        @pl.when(z + dz < NZ)
        def _():
            rows = pl.ds(PLACE[dz] * ZROW, ZROW)
            kv[rows, :LAT] = jnp.zeros((ZROW, LAT), jnp.bfloat16)
            kv[rows, LAT:] = tail_tile

    for load in loads[4:]:
        load.wait()
    out_row = lax.broadcasted_iota(jnp.int32, (GROUP_ROWS, GROUP_ROWS), 0)
    in_row = lax.broadcasted_iota(jnp.int32, (GROUP_ROWS, GROUP_ROWS), 1)
    shuffle = ((out_row % ROWS) * GROUP + out_row // ROWS == in_row).astype(jnp.bfloat16)
    for g in range(N_GROUPS):
        block = ql[:, g * GROUP : (g + 1) * GROUP, :].reshape(GROUP_ROWS, LAT)
        q[g * GROUP_ROWS : (g + 1) * GROUP_ROWS, :LAT] = jnp.dot(
            shuffle, block, preferred_element_type=jnp.float32
        ).astype(jnp.bfloat16)
    for j in range(HEADS // 2):
        pair = qr[:, j * 128 : (j + 1) * 128].astype(jnp.float32)
        for odd in (0, 1):
            part = pltpu.roll(pair, ROPE, 1) if odd else pair
            part = jnp.where(lane < ROPE, part, jnp.where(lane == ROPE, 1.0, 0.0))
            h = 2 * j + odd
            q[h * ROWS : (h + 1) * ROWS, LAT:] = part.astype(jnp.bfloat16)

    def on_a(dz):
        @pl.when(z + dz >= NZ)
        def _():
            a_arrival(dz).wait_recv()
            for dy in (1, 3, 2):
                y_copy(dz, dy).start()

    def on_y(dz):
        def go():
            for dy in (1, 3, 2):
                y_copy(dz, dy).wait_recv()
            c_copy(dz).start()

        if dz == 0:
            go()
        else:
            pl.when(z + dz >= NZ)(go)

    on_a(7)
    on_a(1)
    on_y(0)
    on_a(6)
    on_a(2)
    on_a(5)
    on_a(3)
    on_y(7)
    on_y(1)
    on_a(4)
    on_y(6)
    on_y(2)
    on_y(5)
    on_y(3)
    on_y(4)
    c_copy(0).wait_recv()
    for dz in NEAR_FIRST:

        @pl.when(z + dz >= NZ)
        def _():
            c_copy(dz).wait_recv()

    key_slot = lax.broadcasted_iota(jnp.int32, (GROUP_ROWS, ZROW), 1)
    key_index = ((key_slot // ROWS) % NY) * (2 * ROWS) + (key_slot // (NY * ROWS)) * ROWS + key_slot % ROWS
    query_index = (y * 2 + c) * ROWS + lax.broadcasted_iota(jnp.int32, (GROUP_ROWS, ZROW), 0) % ROWS
    seen = key_index <= query_index

    def x_copy(p):
        columns = pl.ds(pl.multiple_of(p * (PIECE * VD), 128), PIECE * VD)
        return pltpu.make_async_remote_copy(
            src_ref=res.at[:, columns],
            dst_ref=out_hbm.at[0, :, columns],
            send_sem=x_send.at[p],
            recv_sem=x_recv.at[p],
            device_id=after,
            device_id_type=MESH,
        )

    @pl.loop(0, N_GROUPS)
    def _(g):
        rows = pl.ds(pl.multiple_of(g * GROUP_ROWS, GROUP_ROWS), GROUP_ROWS)
        scores = lax.dot_general(
            q[rows, :], kv[...], (((1,), (1,)), ((), ())), preferred_element_type=jnp.float32
        )
        scores = jnp.concatenate([jnp.where(seen, scores[:, :ZROW], MASKED), scores[:, ZROW:]], axis=1)
        top = jnp.max(scores, axis=1, keepdims=True)
        terms = jnp.exp2((scores - top) * SCALE_LOG2E)
        total = jnp.sum(terms, axis=1, keepdims=True)
        summed = jnp.dot(terms.astype(jnp.bfloat16), kv[:, :LAT], preferred_element_type=jnp.float32)
        latent = (summed * (1.0 / jnp.maximum(total, 1.0))).astype(jnp.bfloat16)
        vu_load(g).wait()
        for j in range(GROUP // 2):
            maps = vu[pl.ds(g * GROUP + 2 * j, 2)]
            both = jnp.concatenate([maps[0], maps[1]], axis=1)
            wide = jnp.dot(
                latent[2 * j * ROWS : (2 * j + 2) * ROWS], both, preferred_element_type=jnp.float32
            )
            piece = jnp.concatenate([wide[:ROWS, :VD], wide[ROWS:, VD:]], axis=1) * gate
            columns = pl.ds(pl.multiple_of((g * GROUP + 2 * j) * VD, 128), 2 * VD)
            res[:, columns] = piece.astype(jnp.bfloat16)
            if j % 2 == 1:
                x_copy(g * (GROUP // PIECE) + j // 2).start()

    @pl.loop(0, HEADS // PIECE)
    def _(p):
        x_copy(p).wait()

    for t in (1, 2, 3, 4, 5, 6, 7):

        @pl.when(z + t < NZ)
        def _():
            a_copy(t).wait_send()

    for dz in (0,) + NEAR_FIRST:

        def done():
            for dy in (1, 3, 2):
                y_copy(dz, dy).wait_send()
            c_copy(dz).wait_send()

        if dz == 0:
            done()
        else:
            pl.when(z + dz >= NZ)(done)


def on_device(query_latent, query_rope, key_latent, key_rope, positions, router_weight, value_up):
    return pl.pallas_call(
        body,
        out_shape=jax.ShapeDtypeStruct((1, ROWS, HEADS * VD), jnp.bfloat16),
        in_specs=[pl.BlockSpec(memory_space=pltpu.HBM)] * 7,
        out_specs=pl.BlockSpec(memory_space=pltpu.HBM),
        scratch_shapes=[
            pltpu.VMEM((ROWS, HEADS, LAT), jnp.bfloat16),
            pltpu.VMEM((ROWS, HEADS * ROPE), jnp.bfloat16),
            pltpu.VMEM((ROWS, LAT), jnp.bfloat16),
            pltpu.VMEM((ROWS, ROPE), jnp.bfloat16),
            pltpu.VMEM((1, ROWS), jnp.int32),
            pltpu.VMEM((1, ROWS), jnp.float32),
            pltpu.VMEM((HEADS, LAT, VD), jnp.bfloat16),
            pltpu.VMEM((HEADS * ROWS, WIDE), jnp.bfloat16),
            pltpu.VMEM((KEYS, WIDE), jnp.bfloat16),
            pltpu.VMEM((ROWS, HEADS * VD), jnp.bfloat16),
            pltpu.SemaphoreType.DMA((6,)),
            pltpu.SemaphoreType.DMA((N_GROUPS,)),
            pltpu.SemaphoreType.DMA((NZ - 1,)),
            pltpu.SemaphoreType.DMA((NZ - 1,)),
            pltpu.SemaphoreType.DMA((NZ, 3)),
            pltpu.SemaphoreType.DMA((NZ, 3)),
            pltpu.SemaphoreType.DMA((NZ,)),
            pltpu.SemaphoreType.DMA((NZ,)),
            pltpu.SemaphoreType.DMA((HEADS // PIECE,)),
            pltpu.SemaphoreType.DMA((HEADS // PIECE,)),
        ],
        compiler_params=pltpu.CompilerParams(
            collective_id=0, has_side_effects=True, vmem_limit_bytes=48 * 2**20
        ),
        cost_estimate=pl.CostEstimate(flops=2_400_000_000, bytes_accessed=11_000_000, transcendentals=1_048_576),
        name="attend_and_hand_on",
    )(query_latent, query_rope, key_latent, key_rope, positions, router_weight, value_up)


def solution(mesh):
    placed = (
        P("pipe", "seq", None, None),
        P("pipe", "seq", None),
        P("pipe", "seq", None),
        P("pipe", "seq", None),
        P("pipe", "seq"),
        P("pipe", "seq"),
        P("pipe", None, None, None),
    )
    return jax.shard_map(
        on_device, mesh=mesh, in_specs=placed, out_specs=P("pipe", "seq", None), check_vma=False
    )
```

time: 119 us -> 36.9 us (0.31)
  the two profiles are of different devices: /device:TPU:1 before, /device:TPU:225 now
where the time goes in v1:
time: 36.9 us; the launch traced here: 36.7 us
  Pallas kernels  31.1 us (84%)
  local copies, waits for them, and re-layouts  5.55 us (15%)
    pallas_call x1, Pallas kernels, on_device(): pl.pallas_call(body, out_shape=jax.ShapeDtypeStruct((1, ROWS, HEADS * VD)...  31.1 us
    unnamed x13, local copies, waits for them, and re-layouts  5.55 us

profile of v1, /device:TPU:225, one launch (start us, length us, event | category | flops | bytes accessed | tf_op | source)
XLA Modules:
  0.0 36.7 jit_solution(6433555524440218804)
XLA Ops:
  0.0 0.0 copy-start
  0.0 1.2 %copy-done = bf16[1,16,64,512]{3,2,1,0:T(8,128)(2,1)S(1)} copy-done((bf16[1,16,64,512]{3,2,1,0:T(8,128)(2,1)S(1)}, bf16[1,16,64,512]{3,2,1,0:T(8,128)(2,1)}, u32[]{:S(2)}) %copy-start) | copy-done | bytes 1048600
  1.2 0.0 copy-start.1
  1.2 0.9 %copy-done.1 = bf16[1,16,4096]{2,1,0:T(8,128)(2,1)S(1)} copy-done((bf16[1,16,4096]{2,1,0:T(8,128)(2,1)S(1)}, bf16[1,16,4096]{2,1,0:T(8,128)(2,1)}, u32[]{:S(2)}) %copy-start.1) | copy-done | bytes 131096
  2.1 0.0 copy-start.2
  2.1 0.7 %copy-done.2 = bf16[1,16,512]{2,1,0:T(8,128)(2,1)S(1)} copy-done((bf16[1,16,512]{2,1,0:T(8,128)(2,1)S(1)}, bf16[1,16,512]{2,1,0:T(8,128)(2,1)}, u32[]{:S(2)}) %copy-start.2) | copy-done | bytes 16408
  2.8 0.0 copy-start.3
  2.9 0.7 %copy-done.3 = bf16[1,16,64]{2,1,0:T(8,128)(2,1)S(1)} copy-done((bf16[1,16,64]{2,1,0:T(8,128)(2,1)S(1)}, bf16[1,16,64]{2,1,0:T(8,128)(2,1)}, u32[]{:S(2)}) %copy-start.3) | copy-done | bytes 2072
  3.5 0.0 copy-start.4
  3.5 0.7 %copy-done.4 = s32[1,16]{1,0:T(1,128)S(1)} copy-done((s32[1,16]{1,0:T(1,128)S(1)}, s32[1,16]{1,0:T(1,128)}, u32[]{:S(2)}) %copy-start.4) | copy-done | bytes 88
  4.2 0.0 copy-start.5
  4.2 0.7 %copy-done.5 = f32[1,16]{1,0:T(1,128)S(1)} copy-done((f32[1,16]{1,0:T(1,128)S(1)}, f32[1,16]{1,0:T(1,128)}, u32[]{:S(2)}) %copy-start.5) | copy-done | bytes 88
  4.8 31.1 %attend_and_hand_on.1 = bf16[1,16,8192]{2,1,0:T(8,128)(2,1)S(1)} custom-call(bf16[1,16,64,512]{3,2,1,0:T(8,128)(2,1)S(1)} %copy-done, bf16[1,16,4096]{2,1,0:T(8,128)(2,1)S(1)} %copy-done.1, bf16[1,16,512]{2,1,0:T(8,128)(2,1)S(1)} %copy-done.2, bf16[1,16,64]{2,1,0:T(8,128)(2,1)S(1)} %copy-done.3, s32[1,16]{1,0:T(1,128)S(1)} %copy-done.4, ...), custom_call_target="tpu_custom_call" | custom-call | flops 2400000000 | bytes 11000000 | tf_op jit(solution)/shard_map/attend_and_hand_on/pallas_call | solution.py:288
  36.0 0.7 %copy.9 = bf16[1,16,8192]{2,1,0:T(8,128)(2,1)} copy(bf16[1,16,8192]{2,1,0:T(8,128)(2,1)S(1)} %attend_and_hand_on.1) | data formatting | bytes 524288
Async XLA Ops:
  0.0 1.2 %copy-start = (bf16[1,16,64,512]{3,2,1,0:T(8,128)(2,1)S(1)}, bf16[1,16,64,512]{3,2,1,0:T(8,128)(2,1)}, u32[]{:S(2)}) copy-start(bf16[1,16,64,512]{3,2,1,0:T(8,128)(2,1)} %ql_hbm.1) | copy-start | bytes 3145732
  1.2 0.9 %copy-start.1 = (bf16[1,16,4096]{2,1,0:T(8,128)(2,1)S(1)}, bf16[1,16,4096]{2,1,0:T(8,128)(2,1)}, u32[]{:S(2)}) copy-start(bf16[1,16,4096]{2,1,0:T(8,128)(2,1)} %qr_hbm.1) | copy-start | bytes 393220
  2.1 0.7 %copy-start.2 = (bf16[1,16,512]{2,1,0:T(8,128)(2,1)S(1)}, bf16[1,16,512]{2,1,0:T(8,128)(2,1)}, u32[]{:S(2)}) copy-start(bf16[1,16,512]{2,1,0:T(8,128)(2,1)} %kl_hbm.1) | copy-start | bytes 49156
  2.8 0.7 %copy-start.3 = (bf16[1,16,64]{2,1,0:T(8,128)(2,1)S(1)}, bf16[1,16,64]{2,1,0:T(8,128)(2,1)}, u32[]{:S(2)}) copy-start(bf16[1,16,64]{2,1,0:T(8,128)(2,1)} %kr_hbm.1) | copy-start | bytes 6148
  3.5 0.7 %copy-start.4 = (s32[1,16]{1,0:T(1,128)S(1)}, s32[1,16]{1,0:T(1,128)}, u32[]{:S(2)}) copy-start(s32[1,16]{1,0:T(1,128)} %pos_hbm.1) | copy-start | bytes 196
  4.2 0.7 %copy-start.5 = (f32[1,16]{1,0:T(1,128)S(1)}, f32[1,16]{1,0:T(1,128)}, u32[]{:S(2)}) copy-start(f32[1,16]{1,0:T(1,128)} %rw_hbm.1) | copy-start | bytes 196

commit v2 on v1

--- a/solution.py
+++ b/solution.py
@@ -24,11 +24,13 @@
 MESH = pl.DeviceIdType.MESH
 PLACE = {0: 0, 7: 1, 1: 2, 6: 3, 2: 4, 5: 5, 3: 6, 4: 7}
 NEAR_FIRST = (7, 1, 6, 2, 5, 3, 4)
+FAR = (4, 3, 5, 2, 6)
+EARLY = 4 * ZROW
 
 
 def body(
-    ql_hbm, qr_hbm, kl_hbm, kr_hbm, pos_hbm, rw_hbm, vu_hbm, out_hbm,
-    ql, qr, kl, kr, pos, rw, vu, q, kv, res,
+    ql_hbm, qr_hbm, kl_hbm, kr_hbm, pos_hbm, rw_hbm, vu_hbm, out,
+    ql, qr, kl, kr, pos, rw, vu, q, kv, res, early,
     local_sem, vu_sem, a_send, a_recv, y_send, y_recv, c_send, c_recv, x_send, x_recv,
 ):
     seq = lax.axis_index("seq")
@@ -112,6 +114,26 @@
             device_id_type=MESH,
         )
 
+    def d_copy(t):
+        return pltpu.make_async_remote_copy(
+            src_ref=kv.at[half_of(0, c)],
+            dst_ref=kv.at[half_of(NZ - t, c)],
+            send_sem=a_send.at[t - 1],
+            recv_sem=a_recv.at[NZ - t - 1],
+            device_id=at(z + t, y, c),
+            device_id_type=MESH,
+        )
+
+    def d_arrival(dz):
+        return pltpu.make_async_remote_copy(
+            src_ref=kv.at[half_of(0, c)],
+            dst_ref=kv.at[half_of(dz, c)],
+            send_sem=a_send.at[0],
+            recv_sem=a_recv.at[dz - 1],
+            device_id=sibling,
+            device_id_type=MESH,
+        )
+
     def a_arrival(dz):
         return pltpu.make_async_remote_copy(
             src_ref=kv.at[own_rows],
@@ -142,7 +164,7 @@
             device_id_type=MESH,
         )
 
-    for t in (1, 2, 3, 4, 5, 6, 7):
+    for t in FAR:
 
         @pl.when(z + t < NZ)
         def _():
@@ -188,37 +210,46 @@
                 y_copy(dz, dy).start()
 
     def on_y(dz):
-        def go():
+        @pl.when(z + dz >= NZ)
+        def _():
             for dy in (1, 3, 2):
                 y_copy(dz, dy).wait_recv()
             c_copy(dz).start()
 
-        if dz == 0:
-            go()
-        else:
-            pl.when(z + dz >= NZ)(go)
-
-    on_a(7)
-    on_a(1)
-    on_y(0)
-    on_a(6)
-    on_a(2)
-    on_a(5)
-    on_a(3)
-    on_y(7)
-    on_y(1)
-    on_a(4)
-    on_y(6)
-    on_y(2)
-    on_y(5)
-    on_y(3)
-    on_y(4)
+    def on_d(dz):
+        @pl.when(z + dz >= NZ)
+        def _():
+            d_arrival(dz).wait_recv()
+            c_copy(dz).start()
+
+    def on_c(dz):
+        @pl.when(z + dz >= NZ)
+        def _():
+            c_copy(dz).wait_recv()
+
+    for dy in (1, 3, 2):
+        y_copy(0, dy).wait_recv()
+    for t in (1, 7):
+
+        @pl.when(z + t < NZ)
+        def _():
+            d_copy(t).start()
+
+    c_copy(0).start()
+    for dz in (6, 2, 5, 3, 4):
+        on_a(dz)
+    on_d(7)
+    on_d(1)
+    for dz in (6, 2, 5, 3, 4):
+        on_y(dz)
     c_copy(0).wait_recv()
-    for dz in NEAR_FIRST:
-
-        @pl.when(z + dz >= NZ)
-        def _():
-            c_copy(dz).wait_recv()
+    for dz in (7, 1, 6):
+        on_c(dz)
+    early[...] = lax.dot_general(
+        q[...], kv[:EARLY], (((1,), (1,)), ((), ())), preferred_element_type=jnp.float32
+    )
+    for dz in (2, 5, 3, 4):
+        on_c(dz)
 
     key_slot = lax.broadcasted_iota(jnp.int32, (GROUP_ROWS, ZROW), 1)
     key_index = ((key_slot // ROWS) % NY) * (2 * ROWS) + (key_slot // (NY * ROWS)) * ROWS + key_slot % ROWS
@@ -229,26 +260,30 @@
         columns = pl.ds(pl.multiple_of(p * (PIECE * VD), 128), PIECE * VD)
         return pltpu.make_async_remote_copy(
             src_ref=res.at[:, columns],
-            dst_ref=out_hbm.at[0, :, columns],
+            dst_ref=out.at[0, :, columns],
             send_sem=x_send.at[p],
             recv_sem=x_recv.at[p],
             device_id=after,
             device_id_type=MESH,
         )
 
+    for g in range(N_GROUPS):
+        vu_load(g).wait()
+
     @pl.loop(0, N_GROUPS)
     def _(g):
         rows = pl.ds(pl.multiple_of(g * GROUP_ROWS, GROUP_ROWS), GROUP_ROWS)
-        scores = lax.dot_general(
-            q[rows, :], kv[...], (((1,), (1,)), ((), ())), preferred_element_type=jnp.float32
-        )
-        scores = jnp.concatenate([jnp.where(seen, scores[:, :ZROW], MASKED), scores[:, ZROW:]], axis=1)
+        late = lax.dot_general(
+            q[rows, :], kv[EARLY:], (((1,), (1,)), ((), ())), preferred_element_type=jnp.float32
+        )
+        scores = jnp.concatenate(
+            [jnp.where(seen, early[rows, :ZROW], MASKED), early[rows, ZROW:], late], axis=1
+        )
         top = jnp.max(scores, axis=1, keepdims=True)
         terms = jnp.exp2((scores - top) * SCALE_LOG2E)
         total = jnp.sum(terms, axis=1, keepdims=True)
         summed = jnp.dot(terms.astype(jnp.bfloat16), kv[:, :LAT], preferred_element_type=jnp.float32)
         latent = (summed * (1.0 / jnp.maximum(total, 1.0))).astype(jnp.bfloat16)
-        vu_load(g).wait()
         for j in range(GROUP // 2):
             maps = vu[pl.ds(g * GROUP + 2 * j, 2)]
             both = jnp.concatenate([maps[0], maps[1]], axis=1)
@@ -265,31 +300,37 @@
     def _(p):
         x_copy(p).wait()
 
-    for t in (1, 2, 3, 4, 5, 6, 7):
+    for t in FAR:
 
         @pl.when(z + t < NZ)
         def _():
             a_copy(t).wait_send()
 
-    for dz in (0,) + NEAR_FIRST:
-
-        def done():
-            for dy in (1, 3, 2):
-                y_copy(dz, dy).wait_send()
+    for t in (1, 7):
+
+        @pl.when(z + t < NZ)
+        def _():
+            d_copy(t).wait_send()
+
+    for dy in (1, 3, 2):
+        y_copy(0, dy).wait_send()
+    c_copy(0).wait_send()
+    for dz in NEAR_FIRST:
+
+        @pl.when(z + dz >= NZ)
+        def _():
+            if dz in FAR:
+                for dy in (1, 3, 2):
+                    y_copy(dz, dy).wait_send()
             c_copy(dz).wait_send()
-
-        if dz == 0:
-            done()
-        else:
-            pl.when(z + dz >= NZ)(done)
 
 
 def on_device(query_latent, query_rope, key_latent, key_rope, positions, router_weight, value_up):
     return pl.pallas_call(
         body,
-        out_shape=jax.ShapeDtypeStruct((1, ROWS, HEADS * VD), jnp.bfloat16),
+        out_shape=pltpu.VMEM((1, ROWS, HEADS * VD), jnp.bfloat16),
         in_specs=[pl.BlockSpec(memory_space=pltpu.HBM)] * 7,
-        out_specs=pl.BlockSpec(memory_space=pltpu.HBM),
+        out_specs=pl.BlockSpec(memory_space=pltpu.VMEM),
         scratch_shapes=[
             pltpu.VMEM((ROWS, HEADS, LAT), jnp.bfloat16),
             pltpu.VMEM((ROWS, HEADS * ROPE), jnp.bfloat16),
@@ -301,6 +342,7 @@
             pltpu.VMEM((HEADS * ROWS, WIDE), jnp.bfloat16),
             pltpu.VMEM((KEYS, WIDE), jnp.bfloat16),
             pltpu.VMEM((ROWS, HEADS * VD), jnp.bfloat16),
+            pltpu.VMEM((HEADS * ROWS, EARLY), jnp.float32),
             pltpu.SemaphoreType.DMA((6,)),
             pltpu.SemaphoreType.DMA((N_GROUPS,)),
             pltpu.SemaphoreType.DMA((NZ - 1,)),
@@ -313,7 +355,7 @@
             pltpu.SemaphoreType.DMA((HEADS // PIECE,)),
         ],
         compiler_params=pltpu.CompilerParams(
-            collective_id=0, has_side_effects=True, vmem_limit_bytes=48 * 2**20
+            collective_id=0, has_side_effects=True, vmem_limit_bytes=56 * 2**20
         ),
         cost_estimate=pl.CostEstimate(flops=2_400_000_000, bytes_accessed=11_000_000, transcendentals=1_048_576),
         name="attend_and_hand_on",

time: 36.9 us -> 29.6 us (0.80)
  the two profiles are of different devices: /device:TPU:225 before, /device:TPU:192 now
where the time goes in v2:
time: 29.6 us; the launch traced here: 29.5 us
  Pallas kernels  28.8 us (97%)
  local copies, waits for them, and re-layouts  0.71 us (2%)
    pallas_call x1, Pallas kernels, on_device(): pl.pallas_call(body, out_shape=pltpu.VMEM((1, ROWS, HEADS * VD), jnp.bflo...  28.8 us
    unnamed x1, local copies, waits for them, and re-layouts  0.71 us

profile of v2, /device:TPU:192, one launch (start us, length us, event | category | flops | bytes accessed | tf_op | source)
XLA Modules:
  0.0 29.5 jit_solution(18388459981405463654)
XLA Ops:
  0.0 28.8 %attend_and_hand_on.1 = bf16[1,16,8192]{2,1,0:T(8,128)(2,1)S(1)} custom-call(bf16[1,16,64,512]{3,2,1,0:T(8,128)(2,1)} %ql_hbm.1, bf16[1,16,4096]{2,1,0:T(8,128)(2,1)} %qr_hbm.1, bf16[1,16,512]{2,1,0:T(8,128)(2,1)} %kl_hbm.1, bf16[1,16,64]{2,1,0:T(8,128)(2,1)} %kr_hbm.1, s32[1,16]{1,0:T(1,128)} %pos_hbm.1, f32[1,16]{1,0:T(1,128)} %rw_hbm.1, ...), custom_call_target="tpu_custom_call" | custom-call | flops 2400000000 | bytes 11000000 | tf_op jit(solution)/shard_map/attend_and_hand_on/pallas_call | solution.py:329
  28.8 0.7 %copy.9 = bf16[1,16,8192]{2,1,0:T(8,128)(2,1)} copy(bf16[1,16,8192]{2,1,0:T(8,128)(2,1)S(1)} %attend_and_hand_on.1) | data formatting | bytes 524288

commit v3 on v2

--- a/solution.py
+++ b/solution.py
@@ -20,17 +20,17 @@
 GROUP = 16
 GROUP_ROWS = GROUP * ROWS
 N_GROUPS = HEADS // GROUP
-PIECE = 4
+PIECE = 16
 MESH = pl.DeviceIdType.MESH
 PLACE = {0: 0, 7: 1, 1: 2, 6: 3, 2: 4, 5: 5, 3: 6, 4: 7}
 NEAR_FIRST = (7, 1, 6, 2, 5, 3, 4)
-FAR = (4, 3, 5, 2, 6)
+FAR = (2, 6, 3, 5, 4)
 EARLY = 4 * ZROW
 
 
 def body(
     ql_hbm, qr_hbm, kl_hbm, kr_hbm, pos_hbm, rw_hbm, vu_hbm, out,
-    ql, qr, kl, kr, pos, rw, vu, q, kv, res, early,
+    ql, qr, kl, kr, pos, rw, vu, q, kv, res, early, latents,
     local_sem, vu_sem, a_send, a_recv, y_send, y_recv, c_send, c_recv, x_send, x_recv,
 ):
     seq = lax.axis_index("seq")
@@ -50,7 +50,7 @@
     before = {"pipe": (pipe + 3) % 4}
 
     barrier = pltpu.get_barrier_semaphore()
-    for t in range(1, NZ):
+    for t in (7, 6, 5, 4, 3, 2, 1):
 
         @pl.when(z - t >= 0)
         def _():
@@ -96,85 +96,6 @@
         jnp.where(lane == ROPE, bias, 0.0),
     ).astype(jnp.bfloat16)
 
-    pl.semaphore_wait(barrier, (NZ - 1 - z) + 5)
-
-    def rows_of(dz):
-        return pl.ds(pl.multiple_of(PLACE[dz] * ZROW + place, ROWS), ROWS)
-
-    def half_of(dz, cc):
-        return pl.ds(pl.multiple_of(PLACE[dz] * ZROW + cc * (NY * ROWS), ROWS), NY * ROWS)
-
-    def a_copy(t):
-        return pltpu.make_async_remote_copy(
-            src_ref=kv.at[own_rows],
-            dst_ref=kv.at[rows_of(NZ - t)],
-            send_sem=a_send.at[t - 1],
-            recv_sem=a_recv.at[NZ - t - 1],
-            device_id=at(z + t, y, c),
-            device_id_type=MESH,
-        )
-
-    def d_copy(t):
-        return pltpu.make_async_remote_copy(
-            src_ref=kv.at[half_of(0, c)],
-            dst_ref=kv.at[half_of(NZ - t, c)],
-            send_sem=a_send.at[t - 1],
-            recv_sem=a_recv.at[NZ - t - 1],
-            device_id=at(z + t, y, c),
-            device_id_type=MESH,
-        )
-
-    def d_arrival(dz):
-        return pltpu.make_async_remote_copy(
-            src_ref=kv.at[half_of(0, c)],
-            dst_ref=kv.at[half_of(dz, c)],
-            send_sem=a_send.at[0],
-            recv_sem=a_recv.at[dz - 1],
-            device_id=sibling,
-            device_id_type=MESH,
-        )
-
-    def a_arrival(dz):
-        return pltpu.make_async_remote_copy(
-            src_ref=kv.at[own_rows],
-            dst_ref=kv.at[rows_of(dz)],
-            send_sem=a_send.at[0],
-            recv_sem=a_recv.at[dz - 1],
-            device_id=sibling,
-            device_id_type=MESH,
-        )
-
-    def y_copy(dz, dy):
-        return pltpu.make_async_remote_copy(
-            src_ref=kv.at[rows_of(dz)],
-            dst_ref=kv.at[rows_of(dz)],
-            send_sem=y_send.at[dz, dy - 1],
-            recv_sem=y_recv.at[dz, dy - 1],
-            device_id=y_peer(dy),
-            device_id_type=MESH,
-        )
-
-    def c_copy(dz):
-        return pltpu.make_async_remote_copy(
-            src_ref=kv.at[half_of(dz, c)],
-            dst_ref=kv.at[half_of(dz, c)],
-            send_sem=c_send.at[dz],
-            recv_sem=c_recv.at[dz],
-            device_id=sibling,
-            device_id_type=MESH,
-        )
-
-    for t in FAR:
-
-        @pl.when(z + t < NZ)
-        def _():
-            a_copy(t).start()
-
-    for dy in (1, 3, 2):
-        y_copy(0, dy).start()
-    for g in range(N_GROUPS):
-        vu_load(g).start()
-
     tail_tile = jnp.where(lax.broadcasted_iota(jnp.int32, (ZROW, 128), 1) == ROPE, MASKED, 0.0).astype(jnp.bfloat16)
     for dz in NEAR_FIRST:
 
@@ -202,6 +123,85 @@
             h = 2 * j + odd
             q[h * ROWS : (h + 1) * ROWS, LAT:] = part.astype(jnp.bfloat16)
 
+    pl.semaphore_wait(barrier, (NZ - 1 - z) + 5)
+
+    def rows_of(dz):
+        return pl.ds(pl.multiple_of(PLACE[dz] * ZROW + place, ROWS), ROWS)
+
+    def half_of(dz, cc):
+        return pl.ds(pl.multiple_of(PLACE[dz] * ZROW + cc * (NY * ROWS), ROWS), NY * ROWS)
+
+    def a_copy(t):
+        return pltpu.make_async_remote_copy(
+            src_ref=kv.at[own_rows],
+            dst_ref=kv.at[rows_of(NZ - t)],
+            send_sem=a_send.at[t - 1],
+            recv_sem=a_recv.at[NZ - t - 1],
+            device_id=at(z + t, y, c),
+            device_id_type=MESH,
+        )
+
+    def d_copy(t):
+        return pltpu.make_async_remote_copy(
+            src_ref=kv.at[half_of(0, c)],
+            dst_ref=kv.at[half_of(NZ - t, c)],
+            send_sem=a_send.at[t - 1],
+            recv_sem=a_recv.at[NZ - t - 1],
+            device_id=at(z + t, y, c),
+            device_id_type=MESH,
+        )
+
+    def d_arrival(dz):
+        return pltpu.make_async_remote_copy(
+            src_ref=kv.at[half_of(0, c)],
+            dst_ref=kv.at[half_of(dz, c)],
+            send_sem=a_send.at[0],
+            recv_sem=a_recv.at[dz - 1],
+            device_id=sibling,
+            device_id_type=MESH,
+        )
+
+    def a_arrival(dz):
+        return pltpu.make_async_remote_copy(
+            src_ref=kv.at[own_rows],
+            dst_ref=kv.at[rows_of(dz)],
+            send_sem=a_send.at[0],
+            recv_sem=a_recv.at[dz - 1],
+            device_id=sibling,
+            device_id_type=MESH,
+        )
+
+    def y_copy(dz, dy):
+        return pltpu.make_async_remote_copy(
+            src_ref=kv.at[rows_of(dz)],
+            dst_ref=kv.at[rows_of(dz)],
+            send_sem=y_send.at[dz, dy - 1],
+            recv_sem=y_recv.at[dz, dy - 1],
+            device_id=y_peer(dy),
+            device_id_type=MESH,
+        )
+
+    def c_copy(dz):
+        return pltpu.make_async_remote_copy(
+            src_ref=kv.at[half_of(dz, c)],
+            dst_ref=kv.at[half_of(dz, c)],
+            send_sem=c_send.at[dz],
+            recv_sem=c_recv.at[dz],
+            device_id=sibling,
+            device_id_type=MESH,
+        )
+
+    for t in FAR:
+
+        @pl.when(z + t < NZ)
+        def _():
+            a_copy(t).start()
+
+    for dy in (1, 3, 2):
+        y_copy(0, dy).start()
+    for g in range(N_GROUPS):
+        vu_load(g).start()
+
     def on_a(dz):
         @pl.when(z + dz >= NZ)
         def _():
@@ -273,17 +273,29 @@
     @pl.loop(0, N_GROUPS)
     def _(g):
         rows = pl.ds(pl.multiple_of(g * GROUP_ROWS, GROUP_ROWS), GROUP_ROWS)
-        late = lax.dot_general(
-            q[rows, :], kv[EARLY:], (((1,), (1,)), ((), ())), preferred_element_type=jnp.float32
-        )
-        scores = jnp.concatenate(
-            [jnp.where(seen, early[rows, :ZROW], MASKED), early[rows, ZROW:], late], axis=1
-        )
-        top = jnp.max(scores, axis=1, keepdims=True)
-        terms = jnp.exp2((scores - top) * SCALE_LOG2E)
-        total = jnp.sum(terms, axis=1, keepdims=True)
-        summed = jnp.dot(terms.astype(jnp.bfloat16), kv[:, :LAT], preferred_element_type=jnp.float32)
-        latent = (summed * (1.0 / jnp.maximum(total, 1.0))).astype(jnp.bfloat16)
+
+        def attend(scores, keys):
+            top = jnp.max(scores, axis=1, keepdims=True)
+            terms = jnp.exp2((scores - top) * SCALE_LOG2E)
+            total = jnp.sum(terms, axis=1, keepdims=True)
+            summed = jnp.dot(terms.astype(jnp.bfloat16), kv[:keys, :LAT], preferred_element_type=jnp.float32)
+            latents[...] = (summed * (1.0 / jnp.maximum(total, 1.0))).astype(jnp.bfloat16)
+
+        def first():
+            return jnp.concatenate([jnp.where(seen, early[rows, :ZROW], MASKED), early[rows, ZROW:]], axis=1)
+
+        @pl.when(z >= 3)
+        def _():
+            late = lax.dot_general(
+                q[rows, :], kv[EARLY:], (((1,), (1,)), ((), ())), preferred_element_type=jnp.float32
+            )
+            attend(jnp.concatenate([first(), late], axis=1), KEYS)
+
+        @pl.when(z < 3)
+        def _():
+            attend(first(), EARLY)
+
+        latent = latents[...]
         for j in range(GROUP // 2):
             maps = vu[pl.ds(g * GROUP + 2 * j, 2)]
             both = jnp.concatenate([maps[0], maps[1]], axis=1)
@@ -293,8 +305,8 @@
             piece = jnp.concatenate([wide[:ROWS, :VD], wide[ROWS:, VD:]], axis=1) * gate
             columns = pl.ds(pl.multiple_of((g * GROUP + 2 * j) * VD, 128), 2 * VD)
             res[:, columns] = piece.astype(jnp.bfloat16)
-            if j % 2 == 1:
-                x_copy(g * (GROUP // PIECE) + j // 2).start()
+            if (2 * j + 2) % PIECE == 0:
+                x_copy(g * (GROUP // PIECE) + (2 * j) // PIECE).start()
 
     @pl.loop(0, HEADS // PIECE)
     def _(p):
@@ -343,6 +355,7 @@
             pltpu.VMEM((KEYS, WIDE), jnp.bfloat16),
             pltpu.VMEM((ROWS, HEADS * VD), jnp.bfloat16),
             pltpu.VMEM((HEADS * ROWS, EARLY), jnp.float32),
+            pltpu.VMEM((GROUP_ROWS, LAT), jnp.bfloat16),
             pltpu.SemaphoreType.DMA((6,)),
             pltpu.SemaphoreType.DMA((N_GROUPS,)),
             pltpu.SemaphoreType.DMA((NZ - 1,)),

time: 29.6 us -> 28.6 us (0.966)
  Pallas kernels: 28.8 us -> 27.8 us
    pallas_call x1, Pallas kernels: 28.8 us -> 27.8 us  [on_device(): pl.pallas_call(body, out_shape=pltpu.VMEM((1, ROWS, HEADS * VD), jnp.bflo...]
where the time goes in v3:
time: 28.6 us; the launch traced here: 28.5 us
  Pallas kernels  27.8 us (97%)
  local copies, waits for them, and re-layouts  0.71 us (2%)
    pallas_call x1, Pallas kernels, on_device(): pl.pallas_call(body, out_shape=pltpu.VMEM((1, ROWS, HEADS * VD), jnp.bflo...  27.8 us
    unnamed x1, local copies, waits for them, and re-layouts  0.71 us

profile of v3, /device:TPU:192, one launch (start us, length us, event | category | flops | bytes accessed | tf_op | source)
XLA Modules:
  0.0 28.5 jit_solution(12179352223189515770)
XLA Ops:
  0.0 27.8 %attend_and_hand_on.1 = bf16[1,16,8192]{2,1,0:T(8,128)(2,1)S(1)} custom-call(bf16[1,16,64,512]{3,2,1,0:T(8,128)(2,1)} %ql_hbm.1, bf16[1,16,4096]{2,1,0:T(8,128)(2,1)} %qr_hbm.1, bf16[1,16,512]{2,1,0:T(8,128)(2,1)} %kl_hbm.1, bf16[1,16,64]{2,1,0:T(8,128)(2,1)} %kr_hbm.1, s32[1,16]{1,0:T(1,128)} %pos_hbm.1, f32[1,16]{1,0:T(1,128)} %rw_hbm.1, ...), custom_call_target="tpu_custom_call" | custom-call | flops 2400000000 | bytes 11000000 | tf_op jit(solution)/shard_map/attend_and_hand_on/pallas_call | solution.py:341
  27.8 0.7 %copy.9 = bf16[1,16,8192]{2,1,0:T(8,128)(2,1)} copy(bf16[1,16,8192]{2,1,0:T(8,128)(2,1)S(1)} %attend_and_hand_on.1) | data formatting | bytes 524288

commit v4 on v3

--- a/solution.py
+++ b/solution.py
@@ -24,7 +24,8 @@
 MESH = pl.DeviceIdType.MESH
 PLACE = {0: 0, 7: 1, 1: 2, 6: 3, 2: 4, 5: 5, 3: 6, 4: 7}
 NEAR_FIRST = (7, 1, 6, 2, 5, 3, 4)
-FAR = (2, 6, 3, 5, 4)
+STEPS = (1, 2, 6, 3, 5, 4)
+MID = 4
 EARLY = 4 * ZROW
 
 
@@ -123,6 +124,11 @@
             h = 2 * j + odd
             q[h * ROWS : (h + 1) * ROWS, LAT:] = part.astype(jnp.bfloat16)
 
+    key_slot = lax.broadcasted_iota(jnp.int32, (GROUP_ROWS, ZROW), 1)
+    key_index = ((key_slot // ROWS) % NY) * (2 * ROWS) + (key_slot // (NY * ROWS)) * ROWS + key_slot % ROWS
+    query_index = (y * 2 + c) * ROWS + lax.broadcasted_iota(jnp.int32, (GROUP_ROWS, ZROW), 0) % ROWS
+    seen = key_index <= query_index
+
     pl.semaphore_wait(barrier, (NZ - 1 - z) + 5)
 
     def rows_of(dz):
@@ -191,33 +197,52 @@
             device_id_type=MESH,
         )
 
-    for t in FAR:
-
-        @pl.when(z + t < NZ)
+    def whole(dz, here):
+        if dz == NZ - 1:
+            return here >= MID
+        if dz == 1:
+            return here >= 0
+        if dz == 2:
+            return here < 0
+        if dz == 6:
+            return here < 0
+        return here < 0
+
+    def going(t, half):
+        wanted = whole(NZ - t, z + t)
+        return (z + t < NZ) & (wanted if half else jnp.logical_not(wanted))
+
+    def coming(dz, half):
+        wanted = whole(dz, z)
+        return (z + dz >= NZ) & (wanted if half else jnp.logical_not(wanted))
+
+    for t in STEPS:
+
+        @pl.when(going(t, False))
         def _():
             a_copy(t).start()
 
-    for dy in (1, 3, 2):
+    for dy in (2, 1, 3):
         y_copy(0, dy).start()
     for g in range(N_GROUPS):
         vu_load(g).start()
 
-    def on_a(dz):
-        @pl.when(z + dz >= NZ)
+    def on_a(dz, now=True):
+        @pl.when(coming(dz, False) & now)
         def _():
             a_arrival(dz).wait_recv()
-            for dy in (1, 3, 2):
+            for dy in (2, 1, 3):
                 y_copy(dz, dy).start()
 
-    def on_y(dz):
-        @pl.when(z + dz >= NZ)
-        def _():
-            for dy in (1, 3, 2):
+    def on_y(dz, now=True):
+        @pl.when(coming(dz, False) & now)
+        def _():
+            for dy in (2, 1, 3):
                 y_copy(dz, dy).wait_recv()
             c_copy(dz).start()
 
     def on_d(dz):
-        @pl.when(z + dz >= NZ)
+        @pl.when(coming(dz, True))
         def _():
             d_arrival(dz).wait_recv()
             c_copy(dz).start()
@@ -227,21 +252,31 @@
         def _():
             c_copy(dz).wait_recv()
 
-    for dy in (1, 3, 2):
+    on_a(7)
+    for dy in (2, 1, 3):
         y_copy(0, dy).wait_recv()
-    for t in (1, 7):
-
-        @pl.when(z + t < NZ)
+    for t in (1, 7, 2, 6):
+
+        @pl.when(going(t, True))
         def _():
             d_copy(t).start()
 
     c_copy(0).start()
-    for dz in (6, 2, 5, 3, 4):
+    on_a(6)
+    on_a(4, z == 5)
+    for dz in (5, 2, 3):
         on_a(dz)
+    on_a(4, z != 5)
     on_d(7)
     on_d(1)
-    for dz in (6, 2, 5, 3, 4):
+    for dz in (7, 6, 2):
         on_y(dz)
+    on_d(6)
+    on_d(2)
+    on_y(4, z == 5)
+    for dz in (5, 3):
+        on_y(dz)
+    on_y(4, z != 5)
     c_copy(0).wait_recv()
     for dz in (7, 1, 6):
         on_c(dz)
@@ -250,11 +285,6 @@
     )
     for dz in (2, 5, 3, 4):
         on_c(dz)
-
-    key_slot = lax.broadcasted_iota(jnp.int32, (GROUP_ROWS, ZROW), 1)
-    key_index = ((key_slot // ROWS) % NY) * (2 * ROWS) + (key_slot // (NY * ROWS)) * ROWS + key_slot % ROWS
-    query_index = (y * 2 + c) * ROWS + lax.broadcasted_iota(jnp.int32, (GROUP_ROWS, ZROW), 0) % ROWS
-    seen = key_index <= query_index
 
     def x_copy(p):
         columns = pl.ds(pl.multiple_of(p * (PIECE * VD), 128), PIECE * VD)
@@ -308,33 +338,33 @@
             if (2 * j + 2) % PIECE == 0:
                 x_copy(g * (GROUP // PIECE) + (2 * j) // PIECE).start()
 
+    for t in range(1, NZ):
+
+        @pl.when(going(t, False))
+        def _():
+            a_copy(t).wait_send()
+
+        @pl.when(going(t, True))
+        def _():
+            d_copy(t).wait_send()
+
+    for dy in (2, 1, 3):
+        y_copy(0, dy).wait_send()
+    c_copy(0).wait_send()
+    for dz in NEAR_FIRST:
+
+        @pl.when(z + dz >= NZ)
+        def _():
+            c_copy(dz).wait_send()
+
+        @pl.when(coming(dz, False))
+        def _():
+            for dy in (2, 1, 3):
+                y_copy(dz, dy).wait_send()
+
     @pl.loop(0, HEADS // PIECE)
     def _(p):
         x_copy(p).wait()
-
-    for t in FAR:
-
-        @pl.when(z + t < NZ)
-        def _():
-            a_copy(t).wait_send()
-
-    for t in (1, 7):
-
-        @pl.when(z + t < NZ)
-        def _():
-            d_copy(t).wait_send()
-
-    for dy in (1, 3, 2):
-        y_copy(0, dy).wait_send()
-    c_copy(0).wait_send()
-    for dz in NEAR_FIRST:
-
-        @pl.when(z + dz >= NZ)
-        def _():
-            if dz in FAR:
-                for dy in (1, 3, 2):
-                    y_copy(dz, dy).wait_send()
-            c_copy(dz).wait_send()
 
 
 def on_device(query_latent, query_rope, key_latent, key_rope, positions, router_weight, value_up):

time: 28.6 us -> 28.5 us (level)
  no operation moved by 1% of the time
where the time goes in v4:
time: 28.5 us; the launch traced here: 28.3 us
  Pallas kernels  27.6 us (97%)
  local copies, waits for them, and re-layouts  0.71 us (2%)
    pallas_call x1, Pallas kernels, on_device(): pl.pallas_call(body, out_shape=pltpu.VMEM((1, ROWS, HEADS * VD), jnp.bflo...  27.6 us
    unnamed x1, local copies, waits for them, and re-layouts  0.71 us

profile of v4, /device:TPU:192, one launch (start us, length us, event | category | flops | bytes accessed | tf_op | source)
XLA Modules:
  0.0 28.3 jit_solution(1203284192129323958)
XLA Ops:
  0.0 27.6 %attend_and_hand_on.1 = bf16[1,16,8192]{2,1,0:T(8,128)(2,1)S(1)} custom-call(bf16[1,16,64,512]{3,2,1,0:T(8,128)(2,1)} %ql_hbm.1, bf16[1,16,4096]{2,1,0:T(8,128)(2,1)} %qr_hbm.1, bf16[1,16,512]{2,1,0:T(8,128)(2,1)} %kl_hbm.1, bf16[1,16,64]{2,1,0:T(8,128)(2,1)} %kr_hbm.1, s32[1,16]{1,0:T(1,128)} %pos_hbm.1, f32[1,16]{1,0:T(1,128)} %rw_hbm.1, ...), custom_call_target="tpu_custom_call" | custom-call | flops 2400000000 | bytes 11000000 | tf_op jit(solution)/shard_map/attend_and_hand_on/pallas_call | solution.py:371
  27.6 0.7 %copy.9 = bf16[1,16,8192]{2,1,0:T(8,128)(2,1)} copy(bf16[1,16,8192]{2,1,0:T(8,128)(2,1)S(1)} %attend_and_hand_on.1) | data formatting | bytes 524288

commit v5 on v4

--- a/solution.py
+++ b/solution.py
@@ -216,9 +216,9 @@
         wanted = whole(dz, z)
         return (z + dz >= NZ) & (wanted if half else jnp.logical_not(wanted))
 
-    for t in STEPS:
-
-        @pl.when(going(t, False))
+    for t, now in ((1, True), (2, True), (6, True), (4, z == 2), (3, True), (5, True), (4, z != 2)):
+
+        @pl.when(going(t, False) & now)
         def _():
             a_copy(t).start()
 

time: 28.5 us -> 28.5 us (level)
  no operation moved by 1% of the time
where the time goes in v5:
time: 28.5 us; the launch traced here: 28.1 us
  Pallas kernels  27.4 us (96%)
  local copies, waits for them, and re-layouts  0.71 us (2%)
    pallas_call x1, Pallas kernels, on_device(): pl.pallas_call(body, out_shape=pltpu.VMEM((1, ROWS, HEADS * VD), jnp.bflo...  27.4 us
    unnamed x1, local copies, waits for them, and re-layouts  0.71 us

profile of v5, /device:TPU:192, one launch (start us, length us, event | category | flops | bytes accessed | tf_op | source)
XLA Modules:
  0.0 28.1 jit_solution(2623476914624687480)
XLA Ops:
  0.0 27.4 %attend_and_hand_on.1 = bf16[1,16,8192]{2,1,0:T(8,128)(2,1)S(1)} custom-call(bf16[1,16,64,512]{3,2,1,0:T(8,128)(2,1)} %ql_hbm.1, bf16[1,16,4096]{2,1,0:T(8,128)(2,1)} %qr_hbm.1, bf16[1,16,512]{2,1,0:T(8,128)(2,1)} %kl_hbm.1, bf16[1,16,64]{2,1,0:T(8,128)(2,1)} %kr_hbm.1, s32[1,16]{1,0:T(1,128)} %pos_hbm.1, f32[1,16]{1,0:T(1,128)} %rw_hbm.1, ...), custom_call_target="tpu_custom_call" | custom-call | flops 2400000000 | bytes 11000000 | tf_op jit(solution)/shard_map/attend_and_hand_on/pallas_call | solution.py:371
  27.4 0.7 %copy.9 = bf16[1,16,8192]{2,1,0:T(8,128)(2,1)} copy(bf16[1,16,8192]{2,1,0:T(8,128)(2,1)S(1)} %attend_and_hand_on.1) | data formatting | bytes 524288

commit v6 on v5

--- a/solution.py
+++ b/solution.py
@@ -264,8 +264,10 @@
     c_copy(0).start()
     on_a(6)
     on_a(4, z == 5)
-    for dz in (5, 2, 3):
+    on_a(3, z == 6)
+    for dz in (5, 2):
         on_a(dz)
+    on_a(3, z != 6)
     on_a(4, z != 5)
     on_d(7)
     on_d(1)
@@ -274,8 +276,9 @@
     on_d(6)
     on_d(2)
     on_y(4, z == 5)
-    for dz in (5, 3):
-        on_y(dz)
+    on_y(3, z == 6)
+    on_y(5)
+    on_y(3, z != 6)
     on_y(4, z != 5)
     c_copy(0).wait_recv()
     for dz in (7, 1, 6):

time: 28.5 us -> 28.5 us (level)
  no operation moved by 1% of the time
where the time goes in v6:
time: 28.5 us; the launch traced here: 28.1 us
  Pallas kernels  27.4 us (96%)
  local copies, waits for them, and re-layouts  0.71 us (2%)
    pallas_call x1, Pallas kernels, on_device(): pl.pallas_call(body, out_shape=pltpu.VMEM((1, ROWS, HEADS * VD), jnp.bflo...  27.4 us
    unnamed x1, local copies, waits for them, and re-layouts  0.71 us

profile of v6, /device:TPU:192, one launch (start us, length us, event | category | flops | bytes accessed | tf_op | source)
XLA Modules:
  0.0 28.1 jit_solution(14972031645446318425)
XLA Ops:
  0.0 27.4 %attend_and_hand_on.1 = bf16[1,16,8192]{2,1,0:T(8,128)(2,1)S(1)} custom-call(bf16[1,16,64,512]{3,2,1,0:T(8,128)(2,1)} %ql_hbm.1, bf16[1,16,4096]{2,1,0:T(8,128)(2,1)} %qr_hbm.1, bf16[1,16,512]{2,1,0:T(8,128)(2,1)} %kl_hbm.1, bf16[1,16,64]{2,1,0:T(8,128)(2,1)} %kr_hbm.1, s32[1,16]{1,0:T(1,128)} %pos_hbm.1, f32[1,16]{1,0:T(1,128)} %rw_hbm.1, ...), custom_call_target="tpu_custom_call" | custom-call | flops 2400000000 | bytes 11000000 | tf_op jit(solution)/shard_map/attend_and_hand_on/pallas_call | solution.py:374
  27.4 0.7 %copy.9 = bf16[1,16,8192]{2,1,0:T(8,128)(2,1)} copy(bf16[1,16,8192]{2,1,0:T(8,128)(2,1)S(1)} %attend_and_hand_on.1) | data formatting | bytes 524288
